TPU v7x, 1024 devices: a whole 4x4x32 slice. The times are simulated.
1024 devices in a mesh: dp: 32 (over z_lo, x), expert: 8 (over z_hi, core), tensor: 4 (over y).
Axes of the slice: x: 4, y: 4, z: 32 (z_hi: 4, z_lo: 8; z = z_hi * 8 + z_lo), core: 2. Of those that a mesh axis runs over, the one named last changes fastest.
Arguments:
- residual: bfloat16 [32768, 3072], P(('dp', 'expert'), 'tensor'), parts along dimension 0, may hold values from -40 to 40
- expert_ids: int32 [32768, 4], P(('dp', 'expert')), parts along dimension 0, may hold values from 0 to 15, all different within a row; in each aligned block of 128 rows (0 to 127, 128 to 255, ...) at most 40 rows name the same one
- gate_prob: float32 [32768, 4], P(('dp', 'expert')), parts along dimension 0, may hold values from 0.05 to 1
- expert_hidden: bfloat16 [8, 256, 40, 5632], P('expert', 'dp', None, 'tensor'), parts along dimension 1, may hold values from -6 to 6
- w_down: bfloat16 [8, 5632, 3072], P('expert', 'tensor'), may hold values from -0.078125 to 0.078125
- norm_gain: float32 [3072], P('tensor'), may hold values from 0.1 to 1.9
Outputs:
- normed: bfloat16 [32768, 3072], P(('dp', 'expert'), 'tensor'), parts along dimension 0
There are 32 independent parts, one for each index of `dp`. A program takes and returns all parts, laid end to end along the dimension named above; an argument that names none is the same for every part. Nothing has to cross between parts.
Inputs may be any that keep to these rules, and one draw needn't show every extreme that they name: `expert_ids`: each row names 4 different experts. Within the 128 rows of one index of expert, no expert is named more than 40 times, a bound that some block reaches in some of them.
All inputs are finite; a program needn't handle non-finite values.
Results may differ from a plain program's by a relative error of at most 0.008.
Values may be sent and summed in bfloat16 or wider, within the bound.
No kernel may reach another device: no remote copies, remote signals or barrier semaphores. Data moves between devices by JAX's collectives and lax.ppermute only.
A program may use at most 64 MiB of HBM per device.

v0:
```python
import jax
import jax.numpy as jnp
from jax import lax
from jax.sharding import PartitionSpec as P

EXPERTS = 16


def slot_positions(expert_ids):
    onehot = (expert_ids[..., None] == jnp.arange(EXPERTS, dtype=jnp.int32)).astype(jnp.int32)
    named_count = jnp.sum(onehot, axis=-2)
    prefix = jnp.cumsum(named_count, axis=-2) - named_count
    return jnp.take_along_axis(prefix, expert_ids, axis=-1)


def body(residual, expert_ids, gate_prob, expert_hidden, w_down, norm_gain):
    experts_here = lax.axis_size("expert")
    groups = lax.axis_size("tensor")
    capacity = expert_hidden.shape[2]
    model_width = w_down.shape[2]
    positions = slot_positions(expert_ids)
    in_window = expert_ids < experts_here
    slot_index = jnp.where(in_window, expert_ids * capacity + positions, 0)
    weight = jnp.where(in_window, gate_prob, jnp.float32(0.0))
    hidden = expert_hidden[0].reshape(experts_here * capacity, expert_hidden.shape[3])
    down = w_down[0]
    product = jnp.dot(hidden, down, preferred_element_type=jnp.float32)
    quarter = model_width // groups
    partial_value = product.astype(jnp.bfloat16).reshape(experts_here, capacity, groups, quarter)
    partial_value = jnp.transpose(partial_value, (0, 2, 1, 3)).reshape(
        experts_here * groups, capacity, quarter
    )
    received = lax.all_to_all(
        partial_value, ("expert", "tensor"), split_axis=0, concat_axis=0, tiled=True
    )
    expert_rows = jnp.sum(
        received.reshape(experts_here, groups, capacity, quarter).astype(jnp.float32), axis=1
    )
    picked = jnp.take(expert_rows.reshape(experts_here * capacity, quarter), slot_index, axis=0)
    moe = jnp.sum(picked * weight[..., None], axis=1)
    stream = moe + residual.astype(jnp.float32)
    square_total = lax.psum(jnp.sum(stream * stream, axis=1), "tensor")
    inverse_rms = lax.rsqrt(square_total[:, None] / model_width + 1e-05)
    return (stream * inverse_rms * norm_gain).astype(jnp.bfloat16)


def solution(mesh):
    placed = (
        P(("dp", "expert"), "tensor"),
        P(("dp", "expert"), None),
        P(("dp", "expert"), None),
        P("expert", "dp", None, "tensor"),
        P("expert", "tensor", None),
        P("tensor"),
    )
    return jax.shard_map(
        body, mesh=mesh, in_specs=placed, out_specs=P(("dp", "expert"), "tensor"), check_vma=False
    )
```

profile of v0, /device:TPU:100, one launch (start us, length us, event | category | flops | bytes accessed | tf_op | source)
XLA Modules:
  0.0 251.4 jit_solution(1905470287863876321)
XLA Ops:
  0.0 0.0 copy-start
  0.0 1.2 copy-done
  1.2 8.0 %fusion.2 = bf16[320,3072]{1,0:T(8,128)(2,1)} fusion(bf16[320,1408]{1,0:T(8,128)(2,1)S(1)} %bitcast.18, bf16[1,1408,3072]{2,1,0:T(8,128)(2,1)} %param.10), kind=kOutput, calls=%fused_computation.4 | convolution fusion | flops 2769223680 | bytes 11517952 | tf_op jit(solution)/shard_map/dot_general | solution.py:27
  9.1 3.8 %reshape.34 = bf16[8,40,4,768]{3,2,1,0:T(4,128)(2,1)S(1)} reshape(bf16[320,3072]{1,0:T(8,128)(2,1)} %fusion.2) | data formatting | bytes 3932160 | tf_op jit(solution)/shard_map/reshape | solution.py:29
  12.9 1.5 copy.54
  14.5 0.0 copy-start.2
  14.5 28.9 %all-to-all-start = ((bf16[32,40,768]{2,1,0:T(8,128)(2,1)}), bf16[32,40,768]{2,1,0:T(8,128)(2,1)}, u32[]{:S(2)}, u32[]{:S(2)}) async-start(bf16[32,40,768]{2,1,0:T(8,128)(2,1)} %bitcast.4), calls=%async_computation | async-start | bytes 3932160 | tf_op jit(solution)/shard_map/all_to_all | solution.py:33
  43.4 0.0 copy-done.2
  43.4 0.1 copy.49
  43.5 0.2 reduce_window_sum.11
  43.7 0.1 copy.51
  43.8 0.1 reshape.46
  43.9 0.0 copy-start.4
  43.9 3.8 %gather_fusion.1 = s32[512]{0:T(512)S(1)} fusion(s32[128,16]{1,0:T(8,128)S(1)} %sub.3, s32[512]{0:T(512)S(1)} %reshape.46), kind=kCustom, calls=%fused_computation.1 | custom fusion | bytes 8192 | tf_op jit(solution)/shard_map/jit(take_along_axis)/gather | solution.py:13
  47.7 0.1 reshape.49
  47.8 0.1 copy.52
  47.9 0.1 copy.55
  48.0 0.1 reshape.40
  48.1 0.0 copy-done.4
  48.2 0.1 copy.56
  48.3 0.1 copy.53
  48.4 183.7 %all-to-all-done = bf16[32,40,768]{2,1,0:T(8,128)(2,1)} async-done(((bf16[32,40,768]{2,1,0:T(8,128)(2,1)}), bf16[32,40,768]{2,1,0:T(8,128)(2,1)}, u32[]{:S(2)}, u32[]{:S(2)}) %all-to-all-start) | async-done | bytes 1966112 | tf_op jit(solution)/shard_map/all_to_all | solution.py:33
  232.2 1.9 convert_reduce_fusion
  234.1 2.6 %gather_fusion = f32[512,768]{1,0:T(8,128)} fusion(f32[320,768]{1,0:T(8,128)S(1)} %bitcast.19, s32[1024]{0:T(1024)S(1)} %pad_clamp_fusion), kind=kCustom, calls=%fused_computation | custom fusion | bytes 3147776 | tf_op jit(solution)/shard_map/jit(_take)/gather | solution.py:39
  236.7 0.0 copy-start.1
  236.7 1.8 reshape.39
  238.5 0.0 copy-start.3
  238.5 1.2 multiply_reduce_fusion
  239.7 0.0 copy-done.1
  239.7 0.1 multiply_reduce_fusion.1
  239.8 10.8 %psum.7 = f32[128]{0:T(128)S(1)} all-reduce(f32[128]{0:T(128)S(1)} %multiply_reduce_fusion.1), channel_id=1, replica_groups=mesh['dp'=32,'expert'=8,'tensor'=4] {'tensor'}, use_global_device_ids=true, to_apply=%region_5.6 | all-reduce | flops 128 | bytes 1024 | tf_op jit(solution)/shard_map/psum | solution.py:42
  250.6 0.0 copy-done.3
  250.6 0.8 multiply_convert_fusion
  (7 shorter events, 0.1 us)
Async XLA Ops:
  0.0 1.2 copy-start
  14.5 28.9 %copy-start.2 = (s32[128,4]{0,1:T(4,128)S(1)}, s32[128,4]{0,1:T(4,128)}, u32[]{:S(2)}) copy-start(s32[128,4]{0,1:T(4,128)} %param.7) | copy-start | bytes 6148
  14.5 217.7 %all-to-all-start = ((bf16[32,40,768]{2,1,0:T(8,128)(2,1)}), bf16[32,40,768]{2,1,0:T(8,128)(2,1)}, u32[]{:S(2)}, u32[]{:S(2)}) async-start(bf16[32,40,768]{2,1,0:T(8,128)(2,1)} %bitcast.4), calls=%async_computation | async-start | bytes 3932160 | tf_op jit(solution)/shard_map/all_to_all | solution.py:33
  43.9 4.2 %copy-start.4 = (f32[128,4]{0,1:T(4,128)S(1)}, f32[128,4]{0,1:T(4,128)}, u32[]{:S(2)}) copy-start(f32[128,4]{0,1:T(4,128)} %param.8) | copy-start | bytes 6148
  236.7 3.0 %copy-start.1 = (bf16[128,768]{1,0:T(8,128)(2,1)S(1)}, bf16[128,768]{1,0:T(8,128)(2,1)}, u32[]{:S(2)}) copy-start(bf16[128,768]{1,0:T(8,128)(2,1)} %param.6) | copy-start | bytes 589828
  238.5 12.1 %copy-start.3 = (f32[768]{0:T(1024)S(1)}, f32[768]{0:T(1024)}, u32[]{:S(2)}) copy-start(f32[768]{0:T(1024)} %param.11) | copy-start | bytes 9220
where the time goes:
time: 252 us; the launch traced here: 251 us
  waiting for transfers between devices  184 us (73%)
  starting transfers between devices  28.9 us (11%)
  local copies, waits for them, and re-layouts  15.6 us (6%)
  blocking collectives  10.8 us (4%)
  matrix products  7.97 us (3%)
  other arithmetic  4.24 us (2%)
    all_to_all x1, waiting for transfers between devices, body(): lax.all_to_all(partial_value, ('expert', 'tensor'), split_axis=0, concat_...  184 us
    all_to_all x1, starting transfers between devices, body(): lax.all_to_all(partial_value, ('expert', 'tensor'), split_axis=0, concat_...  28.9 us
    psum x1, blocking collectives, body(): square_total = lax.psum(jnp.sum(stream * stream, axis=1), 'tensor')  10.8 us
    dot_general x1, matrix products, body(): product = jnp.dot(hidden, down, preferred_element_type=jnp.float32)  7.97 us
    reshape x2, local copies, waits for them, and re-layouts, body(): product.astype(jnp.bfloat16)  5.3 us
  transfers between devices with their start and end apart: 1, of which 1 were waited for; matrix products, arithmetic and copies ran while one was open for 2% of the time, Pallas kernels for 0%

commit v1 on v0

v1 whole, which is shorter than its diff:
```python
import functools

import jax
import jax.numpy as jnp
from jax import lax
from jax.experimental import pallas as pl
from jax.experimental.pallas import tpu as pltpu
from jax.sharding import Mesh
from jax.sharding import PartitionSpec as P

EXPERTS = 16
KEY_STRIDE = 64
EPSILON = 1e-05
VMEM_LIMIT = 32 * 1024 * 1024
DOWN_VMEM_LIMIT = 48 * 1024 * 1024
CORES = 2
FIRST_FLOPS = 40_000_000_000
W_BLOCK = 256
PARTS = ((2,), (1, 3, 0))


def kernel_params(limit=VMEM_LIMIT):
    return pltpu.CompilerParams(vmem_limit_bytes=limit)


def routing_kernel(ids_ref, gate_ref, *refs):
    tables = len(refs) // 3
    tokens, topk = ids_ref.shape
    ids = ids_ref[...]
    gate = gate_ref[...]
    lane = lax.broadcasted_iota(jnp.int32, (tokens, EXPERTS), 1)
    hits = [ids[:, k : k + 1] == lane for k in range(topk)]
    named = functools.reduce(jnp.add, [jnp.where(h, 1.0, 0.0) for h in hits])
    earlier = jnp.where(
        lax.broadcasted_iota(jnp.int32, (tokens, tokens), 1)
        < lax.broadcasted_iota(jnp.int32, (tokens, tokens), 0),
        1.0,
        0.0,
    )
    prefix = jnp.dot(
        earlier.astype(jnp.bfloat16),
        named.astype(jnp.bfloat16),
        preferred_element_type=jnp.float32,
    )
    positions = [
        jnp.sum(jnp.where(hits[k], prefix, 0.0), axis=1, keepdims=True) for k in range(topk)
    ]
    keys = [
        ids[:, k : k + 1] * KEY_STRIDE + positions[k].astype(jnp.int32) for k in range(topk)
    ]
    for key_ref, high_ref, low_ref in zip(refs[:tables], refs[tables::2], refs[tables + 1 :: 2]):
        key_of_slot = key_ref[...]
        table = jnp.zeros((tokens, key_ref.shape[1]), jnp.float32)
        for k in range(topk):
            table = table + jnp.where(keys[k] == key_of_slot, gate[:, k : k + 1], 0.0)
        high = table.astype(jnp.bfloat16)
        high_ref[...] = high
        low_ref[...] = (table - high.astype(jnp.float32)).astype(jnp.bfloat16)


def routing_tables(ids, gate, keys):
    out = pl.pallas_call(
        routing_kernel,
        out_shape=[
            jax.ShapeDtypeStruct((ids.shape[0], key.shape[1]), jnp.bfloat16)
            for key in keys
            for _ in range(2)
        ],
        compiler_params=kernel_params(),
        name="routing_tables",
    )(ids, gate, *keys)
    return list(zip(out[0::2], out[1::2]))


def down_kernel(parts, place_ref, hidden_ref, w_ref, *refs):
    out_refs, refs = refs[: len(parts)], refs[len(parts) :]
    held_refs, (rows_ref, w_held, rows_sem, w_sem, out_sem) = refs[: len(parts)], refs[len(parts) :]
    chips, height, depth = hidden_ref.shape
    blocks, _, width = w_held.shape
    _, groups, _, capacity, quarter = out_refs[0].shape
    per_group = quarter // width
    shifts = [s for part in parts for s in part]
    row_copies = [
        pltpu.make_async_copy(
            hidden_ref.at[lax.rem(place_ref[0] + s, chips)], rows_ref.at[i], rows_sem.at[i]
        )
        for i, s in enumerate(shifts)
    ]

    def w_copy(n):
        columns = pl.ds(pl.multiple_of(n * width, width), width)
        return pltpu.make_async_copy(w_ref.at[:, columns], w_held.at[n], w_sem.at[n])

    def out_copies(g):
        return [
            pltpu.make_async_copy(held.at[:, g], out.at[:, g], out_sem.at[i, g])
            for i, (held, out) in enumerate(zip(held_refs, out_refs))
        ]

    for copy in row_copies:
        copy.start()

    @pl.loop(0, blocks)
    def _(n):
        w_copy(n).start()

    for copy in row_copies:
        copy.wait()
    rows = rows_ref[...].reshape(len(shifts) * height, depth)

    @pl.loop(0, groups)
    def _(g):
        @pl.loop(0, per_group)
        def _(j):
            n = g * per_group + j
            w_copy(n).wait()
            value = jnp.dot(rows, w_held[n], preferred_element_type=jnp.float32)
            columns = pl.ds(pl.multiple_of(j * width, width), width)
            first = 0
            for part, held in zip(parts, held_refs):
                for i in range(len(part)):
                    for core in range(CORES):
                        piece = value[first : first + capacity]
                        held[core, g, i, :, columns] = piece.astype(jnp.bfloat16)
                        first += capacity

        for copy in out_copies(g):
            copy.start()

    @pl.loop(0, groups)
    def _(g):
        for copy in out_copies(g):
            copy.wait()


def down(place, hidden, weights, parts, groups):
    chips, height, depth = hidden.shape
    width = W_BLOCK
    quarter = weights.shape[1] // groups
    capacity = height // CORES
    blocks = weights.shape[1] // width
    shapes = [(CORES, groups, len(part), capacity, quarter) for part in parts]
    rows = sum(map(len, parts)) * height
    anywhere = pl.BlockSpec(memory_space=pl.ANY)
    return pl.pallas_call(
        functools.partial(down_kernel, parts),
        in_specs=[pl.BlockSpec(memory_space=pltpu.SMEM), anywhere, anywhere],
        out_specs=[anywhere] * len(parts),
        out_shape=[jax.ShapeDtypeStruct(shape, jnp.bfloat16) for shape in shapes],
        scratch_shapes=[pltpu.VMEM(shape, jnp.bfloat16) for shape in shapes]
        + [
            pltpu.VMEM((sum(map(len, parts)), height, depth), jnp.bfloat16),
            pltpu.VMEM((blocks, depth, width), jnp.bfloat16),
            pltpu.SemaphoreType.DMA((sum(map(len, parts)),)),
            pltpu.SemaphoreType.DMA((blocks,)),
            pltpu.SemaphoreType.DMA((len(parts), groups)),
        ],
        compiler_params=kernel_params(DOWN_VMEM_LIMIT),
        cost_estimate=pl.CostEstimate(
            flops=2 * rows * depth * quarter * groups,
            bytes_accessed=2 * (weights.size + rows * depth + rows * quarter * groups),
            transcendentals=0,
        ),
        name="down_rows",
    )(place, hidden, weights)


def add_kernel(count, later, part_ref, *refs):
    out_refs = refs[later : later + count]
    groups = part_ref.shape[1]
    for i, out_ref in enumerate(out_refs):
        for core in range(CORES):
            values = [part_ref[core, g, i].astype(jnp.float32) for g in range(groups)]
            out_ref[core] = functools.reduce(jnp.add, values).astype(jnp.bfloat16)


def add_groups(parts, later):
    cores, groups, count, capacity, quarter = parts.shape
    anywhere = pl.BlockSpec(memory_space=pl.ANY)
    whole = pl.BlockSpec(memory_space=pltpu.VMEM)
    out = pl.pallas_call(
        functools.partial(add_kernel, count, len(later)),
        in_specs=[whole] + [anywhere] * len(later),
        out_specs=[whole] * count + [anywhere] * len(later),
        out_shape=[jax.ShapeDtypeStruct((cores, capacity, quarter), jnp.bfloat16)] * count
        + [jax.ShapeDtypeStruct(v.shape, v.dtype) for v in later],
        input_output_aliases={1 + i: count + i for i in range(len(later))},
        compiler_params=kernel_params(),
        cost_estimate=pl.CostEstimate(
            flops=parts.size, bytes_accessed=3 * parts.size, transcendentals=0
        ),
        name="add_groups",
    )(parts, *later)
    return out[:count], out[count:]


def picked(table, piece_refs):
    rows = jnp.concatenate(
        [r[core].astype(jnp.float32) for r in piece_refs for core in range(CORES)], axis=0
    )
    rows = rows.astype(jnp.bfloat16)
    high_ref, low_ref = table
    return jnp.dot(high_ref[...], rows, preferred_element_type=jnp.float32) + jnp.dot(
        low_ref[...], rows, preferred_element_type=jnp.float32
    )


def combine_first_kernel(high_ref, low_ref, residual_ref, *refs):
    refs[-1][...] = picked((high_ref, low_ref), refs[:-1]) + residual_ref[...].astype(jnp.float32)


def combine_first(table, residual, pieces):
    return pl.pallas_call(
        combine_first_kernel,
        out_shape=jax.ShapeDtypeStruct(residual.shape, jnp.float32),
        compiler_params=kernel_params(),
        cost_estimate=pl.CostEstimate(
            flops=FIRST_FLOPS, bytes_accessed=8 * residual.size, transcendentals=0
        ),
        name="combine_first",
    )(*table, residual, *pieces)


def combine_last_kernel(high_ref, low_ref, begun_ref, *refs):
    piece_refs, (stream_ref, square_ref) = refs[:-2], refs[-2:]
    stream = begun_ref[...] + picked((high_ref, low_ref), piece_refs)
    stream_ref[...] = stream
    square = stream * stream
    lanes = stream.shape[0]
    folded = functools.reduce(
        jnp.add, [square[:, i : i + lanes] for i in range(0, square.shape[1], lanes)]
    )
    square_ref[...] = jnp.sum(folded.T, axis=0, keepdims=True)


def combine_last(table, begun, pieces):
    return pl.pallas_call(
        combine_last_kernel,
        out_shape=(
            jax.ShapeDtypeStruct(begun.shape, jnp.float32),
            jax.ShapeDtypeStruct((1, begun.shape[0]), jnp.float32),
        ),
        compiler_params=kernel_params(),
        name="combine_last",
    )(*table, begun, *pieces)


def norm_kernel(width, stream_ref, square_ref, gain_ref, out_ref):
    lanes = stream_ref.shape[0]
    inverse = lax.rsqrt(square_ref[...] / width + EPSILON)
    inverse = jnp.broadcast_to(inverse, (lanes, lanes)).T
    for i in range(0, stream_ref.shape[1], lanes):
        out_ref[:, i : i + lanes] = (
            stream_ref[:, i : i + lanes] * inverse * gain_ref[:, i : i + lanes]
        ).astype(jnp.bfloat16)


def norm(stream, square_total, gain, width):
    return pl.pallas_call(
        functools.partial(norm_kernel, width),
        out_shape=jax.ShapeDtypeStruct(stream.shape, jnp.bfloat16),
        compiler_params=kernel_params(),
        name="norm",
    )(stream, square_total, gain)


def body(residual, expert_ids, gate_prob, expert_hidden, w_down, norm_gain):
    chips = lax.axis_size("chip")
    groups = lax.axis_size("tensor")
    capacity, depth = expert_hidden.shape[2:]
    model_width = w_down.shape[2]
    chip = lax.axis_index("chip")
    place = jnp.stack([chip]).astype(jnp.int32)

    def to_chip(value, shift):
        if shift == 0:
            return value
        return lax.ppermute(value, "chip", [(i, (i + shift) % chips) for i in range(chips)])

    def keys_of(shifts):
        expert = jnp.stack(
            [(chip + chips - s) % chips * CORES + core for s in shifts for core in range(CORES)]
        )
        slot = jnp.arange(capacity, dtype=jnp.int32)
        return (expert[:, None] * KEY_STRIDE + slot[None, :]).reshape(1, -1)

    first, last = (2, 0), (1, 3)
    table_first, table_last = routing_tables(
        expert_ids, gate_prob, [keys_of(first), keys_of(last)]
    )

    hidden = expert_hidden.reshape(chips, CORES * capacity, depth)
    values = down(place, hidden, w_down[0], PARTS, groups)
    pieces = {}
    for part in PARTS:
        value, *values = values
        shape = value.shape
        value = lax.all_to_all(
            value.reshape(CORES * groups, *shape[2:]), ("core", "tensor"), 0, 0, tiled=True
        )
        summed, values = add_groups(value.reshape(shape), values)
        pieces.update((s, to_chip(v, s)) for v, s in zip(summed, part))
    begun = combine_first(table_first, residual, [pieces[s] for s in first])
    stream, squares = combine_last(table_last, begun, [pieces[s] for s in last])
    square_total = lax.psum(squares, "tensor")
    return norm(stream, square_total, norm_gain[None, :], model_width)


def solution(mesh):
    dp, expert, tensor = mesh.devices.shape
    cores = Mesh(
        mesh.devices.reshape(dp, expert // CORES, CORES, tensor), ("dp", "chip", "core", "tensor")
    )
    tokens = ("dp", "chip", "core")
    placed = (
        P(tokens, "tensor"),
        P(tokens, None),
        P(tokens, None),
        P(("chip", "core"), "dp", None, "tensor"),
        P(("chip", "core"), "tensor", None),
        P("tensor"),
    )
    return jax.shard_map(
        body, mesh=cores, in_specs=placed, out_specs=P(tokens, "tensor"), check_vma=False
    )
```

time: 252 us -> 113 us (0.45)
  the two profiles are of different devices: /device:TPU:100 before, /device:TPU:6 now
where the time goes in v1:
time: 113 us
  starting transfers between devices  47.3 us (42%)
  waiting for transfers between devices  28.3 us (25%)
  blocking collectives  24.2 us (21%)
  Pallas kernels  10.8 us (10%)
  local copies, waits for them, and re-layouts  1.6 us (1%)
    ppermute x3, starting transfers between devices, to_chip(): lax.ppermute(value, 'chip', [(i, (i + shift) % chips) for i in range(chip...  43.5 us
    ppermute x3, waiting for transfers between devices, to_chip(): lax.ppermute(value, 'chip', [(i, (i + shift) % chips) for i in range(chip...  28.3 us
    all_to_all x1, blocking collectives, body(): lax.all_to_all(value.reshape(CORES * groups, *shape[2:]), ('core', 'tenso...  13.7 us
    psum x1, blocking collectives, body(): square_total = lax.psum(squares, 'tensor')  10.5 us
    pallas_call x1, Pallas kernels, down(): pl.pallas_call(functools.partial(down_kernel, parts), in_specs=[pl.BlockS...  8.63 us
    all_to_all x1, starting transfers between devices, body(): lax.all_to_all(value.reshape(CORES * groups, *shape[2:]), ('core', 'tenso...  3.72 us
  transfers between devices with their start and end apart: 4, of which 2 were waited for; matrix products, arithmetic and copies ran while one was open for 1% of the time, Pallas kernels for 1%

profile of v1, /device:TPU:6, one launch (start us, length us, event | category | flops | bytes accessed | tf_op | source)
XLA Modules:
  0.0 112.7 jit_solution(7568136520357236626)
XLA Ops:
  0.0 0.0 copy-start
  0.0 1.2 %copy-done = bf16[1,8,40,1408]{3,2,1,0:T(8,128)(2,1)S(1)} copy-done((bf16[1,8,40,1408]{3,2,1,0:T(8,128)(2,1)S(1)}, bf16[1,8,40,1408]{3,2,1,0:T(8,128)(2,1)}, u32[]{:S(2)}) %copy-start) | copy-done | bytes 901144
  1.2 8.6 %down_rows.1 = (bf16[2,4,1,40,768]{4,3,2,1,0:T(8,128)(2,1)S(1)}, bf16[2,4,3,40,768]{4,3,2,1,0:T(8,128)(2,1)}) custom-call(s32[1]{0:T(128)} %bitcast.8.place_ref, bf16[4,80,1408]{2,1,0:T(8,128)(2,1)S(1)} %bitcast.20, bf16[1408,3072]{1,0:T(8,128)(2,1)} %bitcast.21), custom_call_target="tpu_custom_call" | custom-call | flops 2768240640 | bytes 11517952 | tf_op jit(solution)/shard_map/down_rows/pallas_call | solution.py:145
  9.8 13.7 %all_to_all.10 = bf16[8,1,40,768]{3,2,1,0:T(8,128)(2,1)S(1)} all-to-all(bf16[8,1,40,768]{3,2,1,0:T(8,128)(2,1)S(1)} %bitcast.19), channel_id=1, replica_groups=mesh['dp'=32,'chip'=4,'core'=2,'tensor'=4] {'core','tensor'}, dimensions={0} | all-to-all | bytes 983040 | tf_op jit(solution)/shard_map/all_to_all | solution.py:298
  23.5 0.1 add_groups.2
  23.5 0.0 copy-start.3
  23.6 0.0 copy-start.4
  23.6 0.0 copy-start.2
  23.6 3.7 %all-to-all-start.1 = ((bf16[8,3,40,768]{3,2,1,0:T(8,128)(2,1)}), bf16[8,3,40,768]{3,2,1,0:T(8,128)(2,1)S(1)}, u32[]{:S(2)}, u32[]{:S(2)}) async-start(bf16[8,3,40,768]{3,2,1,0:T(8,128)(2,1)} %bitcast.14), calls=%async_computation.1 | async-start | bytes 2949120 | tf_op jit(solution)/shard_map/all_to_all | solution.py:298
  27.3 0.0 copy-start.1
  27.4 0.0 copy-done.3
  27.4 0.1 copy.10.ids_ref
  27.5 0.0 copy-done.4
  27.5 0.1 copy.11.gate_ref
  27.6 0.1 add_multiply_fusion
  27.7 0.1 iota_add_fusion.1
  27.8 0.1 add.104.refs_0_
  27.8 0.1 add_multiply_fusion.1
  27.9 29.0 %collective-permute-start = (bf16[2,40,768]{2,1,0:T(8,128)(2,1)S(1)}, bf16[2,40,768]{2,1,0:T(8,128)(2,1)S(1)}, u32[]{:S(2)}, u32[]{:S(2)}) collective-permute-start(bf16[2,40,768]{2,1,0:T(8,128)(2,1)S(1)} %get-tuple-element.24), channel_id=1, source_target_pairs={{0,16},{8,24},{16,0},{24,8},{1,17},{9,25},{17,1},{25,9},{2,18},{10... | collective-permute-start | bytes 368648 | tf_op jit(solution)/shard_map/ppermute | solution.py:278
  56.9 0.1 iota_add_fusion
  57.0 0.1 add.112.refs_1_
  57.1 0.0 copy-done.2
  57.1 0.6 routing_tables.1
  57.7 0.0 all-to-all-done.1
  57.7 0.2 add_groups.3
  57.9 6.1 %collective-permute-start.1 = (bf16[2,40,768]{2,1,0:T(8,128)(2,1)S(1)}, bf16[2,40,768]{2,1,0:T(8,128)(2,1)S(1)}, u32[]{:S(2)}, u32[]{:S(2)}) collective-permute-start(bf16[2,40,768]{2,1,0:T(8,128)(2,1)S(1)} %get-tuple-element.27), channel_id=1, source_target_pairs={{0,8},{8,16},{16,24},{24,0},{1,9},{9,17},{17,25},{25,1},{2,10},{10... | collective-permute-start | bytes 368648 | tf_op jit(solution)/shard_map/ppermute | solution.py:278
  64.0 8.4 %collective-permute-start.2 = (bf16[2,40,768]{2,1,0:T(8,128)(2,1)S(1)}, bf16[2,40,768]{2,1,0:T(8,128)(2,1)S(1)}, u32[]{:S(2)}, u32[]{:S(2)}) collective-permute-start(bf16[2,40,768]{2,1,0:T(8,128)(2,1)S(1)} %get-tuple-element.28), channel_id=1, source_target_pairs={{0,24},{8,0},{16,8},{24,16},{1,25},{9,1},{17,9},{25,17},{2,26},{10... | collective-permute-start | bytes 368648 | tf_op jit(solution)/shard_map/ppermute | solution.py:278
  72.4 0.0 collective-permute-done.refs_0_
  72.4 0.0 copy-done.1
  72.5 0.3 combine_first.1.begun_ref
  72.7 2.4 %collective-permute-done.1.refs_0_ = bf16[2,40,768]{2,1,0:T(8,128)(2,1)S(1)} collective-permute-done((bf16[2,40,768]{2,1,0:T(8,128)(2,1)S(1)}, bf16[2,40,768]{2,1,0:T(8,128)(2,1)S(1)}, u32[]{:S(2)}, u32[]{:S(2)}) %collective-permute-start.1) | collective-permute-done | bytes 122912 | tf_op jit(solution)/shard_map/ppermute | solution.py:278
  75.1 25.9 %collective-permute-done.2.refs_1_ = bf16[2,40,768]{2,1,0:T(8,128)(2,1)S(1)} collective-permute-done((bf16[2,40,768]{2,1,0:T(8,128)(2,1)S(1)}, bf16[2,40,768]{2,1,0:T(8,128)(2,1)S(1)}, u32[]{:S(2)}, u32[]{:S(2)}) %collective-permute-start.2) | collective-permute-done | bytes 122912 | tf_op jit(solution)/shard_map/ppermute | solution.py:278
  101.0 0.3 combine_last.1
  101.4 10.5 %psum.7.square_ref = f32[1,128]{1,0:T(1,128)S(1)} all-reduce(f32[1,128]{1,0:T(1,128)S(1)} %get-tuple-element.30), channel_id=1, replica_groups=mesh['dp'=32,'chip'=4,'core'=2,'tensor'=4] {'tensor'}, use_global_device_ids=true, to_apply=%region_0.1 | all-reduce | flops 128 | bytes 1024 | tf_op jit(solution)/shard_map/psum | solution.py:305
  111.9 0.8 norm.1
  (1 shorter events, 0.0 us)
Async XLA Ops:
  0.0 1.2 %copy-start = (bf16[1,8,40,1408]{3,2,1,0:T(8,128)(2,1)S(1)}, bf16[1,8,40,1408]{3,2,1,0:T(8,128)(2,1)}, u32[]{:S(2)}) copy-start(bf16[1,8,40,1408]{3,2,1,0:T(8,128)(2,1)} %param.9) | copy-start | bytes 2703364
  23.5 3.8 %copy-start.3 = (s32[128,4]{0,1:T(4,128)S(1)}, s32[128,4]{0,1:T(4,128)}, u32[]{:S(2)}) copy-start(s32[128,4]{0,1:T(4,128)} %param.7) | copy-start | bytes 6148
  23.6 3.9 %copy-start.4 = (f32[128,4]{0,1:T(4,128)S(1)}, f32[128,4]{0,1:T(4,128)}, u32[]{:S(2)}) copy-start(f32[128,4]{0,1:T(4,128)} %param.8) | copy-start | bytes 6148
  23.6 33.5 %copy-start.2 = (f32[768]{0:T(1024)S(1)}, f32[768]{0:T(1024)}, u32[]{:S(2)}) copy-start(f32[768]{0:T(1024)} %param.11) | copy-start | bytes 9220
  23.6 34.1 %all-to-all-start.1 = ((bf16[8,3,40,768]{3,2,1,0:T(8,128)(2,1)}), bf16[8,3,40,768]{3,2,1,0:T(8,128)(2,1)S(1)}, u32[]{:S(2)}, u32[]{:S(2)}) async-start(bf16[8,3,40,768]{3,2,1,0:T(8,128)(2,1)} %bitcast.14), calls=%async_computation.1 | async-start | bytes 2949120 | tf_op jit(solution)/shard_map/all_to_all | solution.py:298
  27.3 45.1 %copy-start.1 = (bf16[128,768]{1,0:T(8,128)(2,1)S(1)}, bf16[128,768]{1,0:T(8,128)(2,1)}, u32[]{:S(2)}) copy-start(bf16[128,768]{1,0:T(8,128)(2,1)} %residual_ref.1) | copy-start | bytes 589828
  27.9 44.5 %collective-permute-start = (bf16[2,40,768]{2,1,0:T(8,128)(2,1)S(1)}, bf16[2,40,768]{2,1,0:T(8,128)(2,1)S(1)}, u32[]{:S(2)}, u32[]{:S(2)}) collective-permute-start(bf16[2,40,768]{2,1,0:T(8,128)(2,1)S(1)} %get-tuple-element.24), channel_id=1, source_target_pairs={{0,16},{8,24},{16,0},{24,8},{1,17},{9,25},{17,1},{25,9},{2,18},{10... | collective-permute-start | bytes 368648 | tf_op jit(solution)/shard_map/ppermute | solution.py:278
  57.9 17.3 %collective-permute-start.1 = (bf16[2,40,768]{2,1,0:T(8,128)(2,1)S(1)}, bf16[2,40,768]{2,1,0:T(8,128)(2,1)S(1)}, u32[]{:S(2)}, u32[]{:S(2)}) collective-permute-start(bf16[2,40,768]{2,1,0:T(8,128)(2,1)S(1)} %get-tuple-element.27), channel_id=1, source_target_pairs={{0,8},{8,16},{16,24},{24,0},{1,9},{9,17},{17,25},{25,1},{2,10},{10... | collective-permute-start | bytes 368648 | tf_op jit(solution)/shard_map/ppermute | solution.py:278
  64.0 37.1 %collective-permute-start.2 = (bf16[2,40,768]{2,1,0:T(8,128)(2,1)S(1)}, bf16[2,40,768]{2,1,0:T(8,128)(2,1)S(1)}, u32[]{:S(2)}, u32[]{:S(2)}) collective-permute-start(bf16[2,40,768]{2,1,0:T(8,128)(2,1)S(1)} %get-tuple-element.28), channel_id=1, source_target_pairs={{0,24},{8,0},{16,8},{24,16},{1,25},{9,1},{17,9},{25,17},{2,26},{10... | collective-permute-start | bytes 368648 | tf_op jit(solution)/shard_map/ppermute | solution.py:278

commit v2 on v1

--- a/solution.py
+++ b/solution.py
@@ -12,11 +12,13 @@
 KEY_STRIDE = 64
 EPSILON = 1e-05
 VMEM_LIMIT = 32 * 1024 * 1024
-DOWN_VMEM_LIMIT = 48 * 1024 * 1024
+DOWN_VMEM_LIMIT = 60 * 1024 * 1024
+HERE_VMEM_LIMIT = 48 * 1024 * 1024
 CORES = 2
 FIRST_FLOPS = 40_000_000_000
-W_BLOCK = 256
-PARTS = ((2,), (1, 3, 0))
+W_BLOCK = 512
+AHEAD = 3
+PARTS = ((2,), (3, 1), (0,))
 
 
 def kernel_params(limit=VMEM_LIMIT):
@@ -73,96 +75,98 @@
 
 
 def down_kernel(parts, place_ref, hidden_ref, w_ref, *refs):
+    refs = refs[len(refs) - 2 * len(parts) - 5 :]
     out_refs, refs = refs[: len(parts)], refs[len(parts) :]
     held_refs, (rows_ref, w_held, rows_sem, w_sem, out_sem) = refs[: len(parts)], refs[len(parts) :]
-    chips, height, depth = hidden_ref.shape
+    chips, height, _ = hidden_ref.shape
     blocks, _, width = w_held.shape
     _, groups, _, capacity, quarter = out_refs[0].shape
-    per_group = quarter // width
     shifts = [s for part in parts for s in part]
     row_copies = [
         pltpu.make_async_copy(
-            hidden_ref.at[lax.rem(place_ref[0] + s, chips)], rows_ref.at[i], rows_sem.at[i]
+            hidden_ref.at[jnp.bitwise_xor(place_ref[0], s)],
+            rows_ref.at[i * height : (i + 1) * height],
+            rows_sem.at[i],
         )
         for i, s in enumerate(shifts)
     ]
-
-    def w_copy(n):
-        columns = pl.ds(pl.multiple_of(n * width, width), width)
-        return pltpu.make_async_copy(w_ref.at[:, columns], w_held.at[n], w_sem.at[n])
-
-    def out_copies(g):
-        return [
+    w_copies = [
+        pltpu.make_async_copy(
+            w_ref.at[:, n * width : (n + 1) * width], w_held.at[n], w_sem.at[n]
+        )
+        for n in range(blocks)
+    ]
+    out_copies = [
+        [
             pltpu.make_async_copy(held.at[:, g], out.at[:, g], out_sem.at[i, g])
             for i, (held, out) in enumerate(zip(held_refs, out_refs))
         ]
-
-    for copy in row_copies:
+        for g in range(groups)
+    ]
+    for copy in row_copies + w_copies[:AHEAD]:
         copy.start()
-
-    @pl.loop(0, blocks)
-    def _(n):
-        w_copy(n).start()
-
     for copy in row_copies:
         copy.wait()
-    rows = rows_ref[...].reshape(len(shifts) * height, depth)
-
-    @pl.loop(0, groups)
-    def _(g):
-        @pl.loop(0, per_group)
-        def _(j):
-            n = g * per_group + j
-            w_copy(n).wait()
-            value = jnp.dot(rows, w_held[n], preferred_element_type=jnp.float32)
-            columns = pl.ds(pl.multiple_of(j * width, width), width)
+    stored = 0
+    for n in range(blocks):
+        w_copies[n].wait()
+        if n + AHEAD < blocks:
+            w_copies[n + AHEAD].start()
+        value = jnp.dot(rows_ref[...], w_held[n], preferred_element_type=jnp.float32)
+        begin, end = n * width, (n + 1) * width
+        left = begin
+        while left < end:
+            g = left // quarter
+            right = min(end, (g + 1) * quarter)
             first = 0
             for part, held in zip(parts, held_refs):
                 for i in range(len(part)):
                     for core in range(CORES):
-                        piece = value[first : first + capacity]
-                        held[core, g, i, :, columns] = piece.astype(jnp.bfloat16)
+                        held[core, g, i, :, left - g * quarter : right - g * quarter] = value[
+                            first : first + capacity, left - begin : right - begin
+                        ].astype(jnp.bfloat16)
                         first += capacity
-
-        for copy in out_copies(g):
-            copy.start()
-
-    @pl.loop(0, groups)
-    def _(g):
-        for copy in out_copies(g):
+            left = right
+        while (stored + 1) * quarter <= end:
+            for copy in out_copies[stored]:
+                copy.start()
+            stored += 1
+    for copies in out_copies:
+        for copy in copies:
             copy.wait()
 
 
-def down(place, hidden, weights, parts, groups):
+def down(place, hidden, weights, parts, groups, limit, after=()):
     chips, height, depth = hidden.shape
     width = W_BLOCK
     quarter = weights.shape[1] // groups
     capacity = height // CORES
     blocks = weights.shape[1] // width
     shapes = [(CORES, groups, len(part), capacity, quarter) for part in parts]
-    rows = sum(map(len, parts)) * height
+    count = sum(map(len, parts))
+    rows = count * height
     anywhere = pl.BlockSpec(memory_space=pl.ANY)
     return pl.pallas_call(
         functools.partial(down_kernel, parts),
-        in_specs=[pl.BlockSpec(memory_space=pltpu.SMEM), anywhere, anywhere],
+        in_specs=[pl.BlockSpec(memory_space=pltpu.SMEM)] + [anywhere] * (2 + len(after)),
         out_specs=[anywhere] * len(parts),
         out_shape=[jax.ShapeDtypeStruct(shape, jnp.bfloat16) for shape in shapes],
         scratch_shapes=[pltpu.VMEM(shape, jnp.bfloat16) for shape in shapes]
         + [
-            pltpu.VMEM((sum(map(len, parts)), height, depth), jnp.bfloat16),
+            pltpu.VMEM((rows, depth), jnp.bfloat16),
             pltpu.VMEM((blocks, depth, width), jnp.bfloat16),
-            pltpu.SemaphoreType.DMA((sum(map(len, parts)),)),
+            pltpu.SemaphoreType.DMA((count,)),
             pltpu.SemaphoreType.DMA((blocks,)),
             pltpu.SemaphoreType.DMA((len(parts), groups)),
         ],
-        compiler_params=kernel_params(DOWN_VMEM_LIMIT),
+        compiler_params=kernel_params(limit),
         cost_estimate=pl.CostEstimate(
             flops=2 * rows * depth * quarter * groups,
             bytes_accessed=2 * (weights.size + rows * depth + rows * quarter * groups),
             transcendentals=0,
         ),
         name="down_rows",
-    )(place, hidden, weights)
+    )(place, hidden, weights, *after)
 
 
 def add_kernel(count, later, part_ref, *refs):
@@ -174,7 +178,7 @@
             out_ref[core] = functools.reduce(jnp.add, values).astype(jnp.bfloat16)
 
 
-def add_groups(parts, later):
+def add_groups(parts, later=()):
     cores, groups, count, capacity, quarter = parts.shape
     anywhere = pl.BlockSpec(memory_space=pl.ANY)
     whole = pl.BlockSpec(memory_space=pltpu.VMEM)
@@ -247,7 +251,8 @@
 
 def norm_kernel(width, stream_ref, square_ref, gain_ref, out_ref):
     lanes = stream_ref.shape[0]
-    inverse = lax.rsqrt(square_ref[...] / width + EPSILON)
+    square_total = jnp.sum(square_ref[...], axis=0, keepdims=True)
+    inverse = lax.rsqrt(square_total / width + EPSILON)
     inverse = jnp.broadcast_to(inverse, (lanes, lanes)).T
     for i in range(0, stream_ref.shape[1], lanes):
         out_ref[:, i : i + lanes] = (
@@ -255,13 +260,13 @@
         ).astype(jnp.bfloat16)
 
 
-def norm(stream, square_total, gain, width):
+def norm(stream, square_parts, gain, width):
     return pl.pallas_call(
         functools.partial(norm_kernel, width),
         out_shape=jax.ShapeDtypeStruct(stream.shape, jnp.bfloat16),
         compiler_params=kernel_params(),
         name="norm",
-    )(stream, square_total, gain)
+    )(stream, square_parts, gain)
 
 
 def body(residual, expert_ids, gate_prob, expert_hidden, w_down, norm_gain):
@@ -273,37 +278,44 @@
     place = jnp.stack([chip]).astype(jnp.int32)
 
     def to_chip(value, shift):
-        if shift == 0:
+        if not shift:
             return value
-        return lax.ppermute(value, "chip", [(i, (i + shift) % chips) for i in range(chips)])
+        return lax.ppermute(value, "chip", [(i, i ^ shift) for i in range(chips)])
 
     def keys_of(shifts):
         expert = jnp.stack(
-            [(chip + chips - s) % chips * CORES + core for s in shifts for core in range(CORES)]
+            [(chip ^ s) * CORES + core for s in shifts for core in range(CORES)]
         )
         slot = jnp.arange(capacity, dtype=jnp.int32)
         return (expert[:, None] * KEY_STRIDE + slot[None, :]).reshape(1, -1)
 
-    first, last = (2, 0), (1, 3)
+    first, last = (2,), (3, 1, 0)
     table_first, table_last = routing_tables(
         expert_ids, gate_prob, [keys_of(first), keys_of(last)]
     )
 
     hidden = expert_hidden.reshape(chips, CORES * capacity, depth)
-    values = down(place, hidden, w_down[0], PARTS, groups)
-    pieces = {}
-    for part in PARTS:
-        value, *values = values
+    weights = w_down[0]
+    far, near, here = PARTS
+    far_value, near_value = down(place, hidden, weights, (far, near), groups, DOWN_VMEM_LIMIT)
+
+    def to_tokens(value, part, later=()):
         shape = value.shape
         value = lax.all_to_all(
             value.reshape(CORES * groups, *shape[2:]), ("core", "tensor"), 0, 0, tiled=True
         )
-        summed, values = add_groups(value.reshape(shape), values)
-        pieces.update((s, to_chip(v, s)) for v, s in zip(summed, part))
+        summed, later = add_groups(value.reshape(shape), later)
+        return summed, later, [(s, to_chip(v, s)) for v, s in zip(summed, part)]
+
+    far_summed, _, far_pieces = to_tokens(far_value, far)
+    here_value = down(place, hidden, weights, (here,), groups, HERE_VMEM_LIMIT, far_summed)
+    _, (here_value,), near_pieces = to_tokens(near_value, near, here_value)
+    _, _, here_pieces = to_tokens(here_value, here)
+    pieces = dict(far_pieces + near_pieces + here_pieces)
     begun = combine_first(table_first, residual, [pieces[s] for s in first])
     stream, squares = combine_last(table_last, begun, [pieces[s] for s in last])
-    square_total = lax.psum(squares, "tensor")
-    return norm(stream, square_total, norm_gain[None, :], model_width)
+    square_parts = lax.all_gather(squares, "tensor", axis=0, tiled=True)
+    return norm(stream, square_parts, norm_gain[None, :], model_width)
 
 
 def solution(mesh):

time: 113 us -> 108 us (0.956)
  waiting for transfers between devices: 28.3 us -> 22.5 us
  Pallas kernels: 10.8 us -> 13.8 us
    ppermute x3, waiting for transfers between devices: 28.3 us -> 13.4 us  [to_chip(): return lax.ppermute(value, 'chip', [(i, i ^ shift) for i in range(chips)])]
    psum x1 -> x0, blocking collectives: 10.5 us -> none  [body(): square_total = lax.psum(squares, 'tensor')]
    all_gather x0 -> x1, blocking collectives: none -> 9.81 us  [body(): square_parts = lax.all_gather(squares, 'tensor', axis=0, tiled=True)]
    all_to_all x1 -> x2, waiting for transfers between devices: 0.01 us -> 9.04 us  [to_tokens(): lax.all_to_all(value.reshape(CORES * groups, *shape[2:]), ('core', 'tenso...]
    ppermute x3, starting transfers between devices: 43.5 us -> 39.3 us  [to_chip(): return lax.ppermute(value, 'chip', [(i, i ^ shift) for i in range(chips)])]
    all_to_all x1 -> x2, starting transfers between devices: 3.72 us -> 7.05 us  [to_tokens(): lax.all_to_all(value.reshape(CORES * groups, *shape[2:]), ('core', 'tenso...]
    pallas_call x1 -> x2, Pallas kernels: 8.63 us -> 11.6 us  [down(): pl.pallas_call(functools.partial(down_kernel, parts), in_specs=[pl.BlockS...]
    unnamed x12, local copies, waits for them, and re-layouts: 1.42 us -> 0.25 us
  transfers between devices with their start and end apart: 4 -> 5, of which waited for: 2 -> 3; matrix products, arithmetic and copies ran while one was open for 1% -> 1% of each run, Pallas kernels for 1% -> 6%
where the time goes in v2:
time: 108 us; the launch traced here: 107 us
  starting transfers between devices  46.4 us (43%)
  blocking collectives  23.8 us (22%)
  waiting for transfers between devices  22.5 us (21%)
  Pallas kernels  13.8 us (13%)
    ppermute x3, starting transfers between devices, to_chip(): return lax.ppermute(value, 'chip', [(i, i ^ shift) for i in range(chips)])  39.3 us
    all_to_all x1, blocking collectives, to_tokens(): lax.all_to_all(value.reshape(CORES * groups, *shape[2:]), ('core', 'tenso...  14 us
    ppermute x3, waiting for transfers between devices, to_chip(): return lax.ppermute(value, 'chip', [(i, i ^ shift) for i in range(chips)])  13.4 us
    pallas_call x2, Pallas kernels, down(): pl.pallas_call(functools.partial(down_kernel, parts), in_specs=[pl.BlockS...  11.6 us
    all_gather x1, blocking collectives, body(): square_parts = lax.all_gather(squares, 'tensor', axis=0, tiled=True)  9.81 us
    all_to_all x2, waiting for transfers between devices, to_tokens(): lax.all_to_all(value.reshape(CORES * groups, *shape[2:]), ('core', 'tenso...  9.04 us
    all_to_all x2, starting transfers between devices, to_tokens(): lax.all_to_all(value.reshape(CORES * groups, *shape[2:]), ('core', 'tenso...  7.05 us
  transfers between devices with their start and end apart: 5, of which 3 were waited for; matrix products, arithmetic and copies ran while one was open for 1% of the time, Pallas kernels for 6%

profile of v2, /device:TPU:6, one launch (start us, length us, event | category | flops | bytes accessed | tf_op | source)
XLA Modules:
  0.0 107.4 jit_solution(14448566811953882239)
XLA Ops:
  0.0 0.0 copy-start
  0.0 0.0 copy-start.3
  0.0 0.0 copy-start.4
  0.0 0.0 copy-start.2
  0.0 6.3 %down_rows.2 = (bf16[2,4,1,40,768]{4,3,2,1,0:T(8,128)(2,1)}, bf16[2,4,2,40,768]{4,3,2,1,0:T(8,128)(2,1)}) custom-call(s32[1]{0:T(128)} %bitcast.8.place_ref, bf16[4,80,1408]{2,1,0:T(8,128)(2,1)} %bitcast.24, bf16[1408,3072]{1,0:T(8,128)(2,1)} %bitcast.30), custom_call_target="tpu_custom_call" | custom-call | flops 2076180480 | bytes 10801152 | tf_op jit(solution)/shard_map/down_rows/pallas_call | solution.py:149
  6.3 0.0 copy-start.1
  6.4 14.0 %all_to_all.15 = bf16[8,1,40,768]{3,2,1,0:T(8,128)(2,1)S(1)} all-to-all(bf16[8,1,40,768]{3,2,1,0:T(8,128)(2,1)} %bitcast.33), channel_id=1, replica_groups=mesh['dp'=32,'chip'=4,'core'=2,'tensor'=4] {'core','tensor'}, dimensions={0} | all-to-all | bytes 983040 | tf_op jit(solution)/shard_map/all_to_all | solution.py:304
  20.4 3.6 %all-to-all-start.1 = ((bf16[8,2,40,768]{3,2,1,0:T(8,128)(2,1)}), bf16[8,2,40,768]{3,2,1,0:T(8,128)(2,1)S(1)}, u32[]{:S(2)}, u32[]{:S(2)}) async-start(bf16[8,2,40,768]{3,2,1,0:T(8,128)(2,1)} %bitcast.32), calls=%async_computation.1 | async-start | bytes 1966080 | tf_op jit(solution)/shard_map/all_to_all | solution.py:304
  23.9 0.1 stack.42
  24.0 0.1 add_multiply_fusion
  24.1 0.1 iota_add_fusion
  24.2 0.1 add_groups.3.refs_0_
  24.2 29.0 %collective-permute-start = (bf16[2,40,768]{2,1,0:T(8,128)(2,1)S(1)}, bf16[2,40,768]{2,1,0:T(8,128)(2,1)S(1)}, u32[]{:S(2)}, u32[]{:S(2)}) collective-permute-start(bf16[2,40,768]{2,1,0:T(8,128)(2,1)S(1)} %add_groups.3.refs_0_), channel_id=1, source_target_pairs={{0,16},{8,24},{16,0},{24,8},{1,17},{9,25},{17,1},{25,9},{2,18},{10... | collective-permute-start | bytes 368648 | tf_op jit(solution)/shard_map/ppermute | solution.py:283
  53.2 0.1 iota_add_fusion.1
  53.3 0.0 copy-done.3
  53.3 0.1 copy.11.ids_ref
  53.4 0.0 copy-done.4
  53.4 0.1 copy.12.gate_ref
  53.5 0.1 add.62.refs_0_
  53.6 0.1 add.69.refs_1_
  53.7 0.0 copy-done.2
  53.7 0.6 routing_tables.1
  54.3 0.0 copy-done
  54.3 5.3 %down_rows.3.refs_0_ = bf16[2,4,1,40,768]{4,3,2,1,0:T(8,128)(2,1)} custom-call(s32[1]{0:T(128)} %bitcast.8.place_ref, bf16[4,80,1408]{2,1,0:T(8,128)(2,1)S(1)} %bitcast.25, bf16[1408,3072]{1,0:T(8,128)(2,1)} %bitcast.31, bf16[2,40,768]{2,1,0:T(8,128)(2,1)S(1)} %add_groups.3.refs_0_), custom_call_target="tpu_custom_call" | custom-call | flops 692060160 | bytes 9367552 | tf_op jit(solution)/shard_map/down_rows/pallas_call | solution.py:149
  59.6 0.0 all-to-all-done.1
  59.6 0.1 add_groups.4
  59.7 1.9 %collective-permute-start.1 = (bf16[2,40,768]{2,1,0:T(8,128)(2,1)S(1)}, bf16[2,40,768]{2,1,0:T(8,128)(2,1)S(1)}, u32[]{:S(2)}, u32[]{:S(2)}) collective-permute-start(bf16[2,40,768]{2,1,0:T(8,128)(2,1)S(1)} %get-tuple-element.22), channel_id=1, source_target_pairs={{0,24},{8,16},{16,8},{24,0},{1,25},{9,17},{17,9},{25,1},{2,26},{10... | collective-permute-start | bytes 368648 | tf_op jit(solution)/shard_map/ppermute | solution.py:283
  61.6 8.4 %collective-permute-start.2 = (bf16[2,40,768]{2,1,0:T(8,128)(2,1)S(1)}, bf16[2,40,768]{2,1,0:T(8,128)(2,1)S(1)}, u32[]{:S(2)}, u32[]{:S(2)}) collective-permute-start(bf16[2,40,768]{2,1,0:T(8,128)(2,1)S(1)} %get-tuple-element.23), channel_id=1, source_target_pairs={{0,8},{8,0},{16,24},{24,16},{1,9},{9,1},{17,25},{25,17},{2,10},{10... | collective-permute-start | bytes 368648 | tf_op jit(solution)/shard_map/ppermute | solution.py:283
  70.1 3.5 %all-to-all-start.2 = ((bf16[8,1,40,768]{3,2,1,0:T(8,128)(2,1)}), bf16[8,1,40,768]{3,2,1,0:T(8,128)(2,1)S(1)}, u32[]{:S(2)}, u32[]{:S(2)}) async-start(bf16[8,1,40,768]{3,2,1,0:T(8,128)(2,1)} %bitcast.17), calls=%async_computation.2 | async-start | bytes 983040 | tf_op jit(solution)/shard_map/all_to_all | solution.py:304
  73.6 0.0 collective-permute-done.refs_0_
  73.6 0.0 copy-done.1
  73.6 0.2 combine_first.1.begun_ref
  73.9 9.0 %all-to-all-done.2 = bf16[8,1,40,768]{3,2,1,0:T(8,128)(2,1)S(1)} async-done(((bf16[8,1,40,768]{3,2,1,0:T(8,128)(2,1)}), bf16[8,1,40,768]{3,2,1,0:T(8,128)(2,1)S(1)}, u32[]{:S(2)}, u32[]{:S(2)}) %all-to-all-start.2) | async-done | bytes 491552 | tf_op jit(solution)/shard_map/all_to_all | solution.py:304
  82.9 0.1 add_groups.5.refs_2_
  83.0 12.6 %collective-permute-done.1.refs_0_ = bf16[2,40,768]{2,1,0:T(8,128)(2,1)S(1)} collective-permute-done((bf16[2,40,768]{2,1,0:T(8,128)(2,1)S(1)}, bf16[2,40,768]{2,1,0:T(8,128)(2,1)S(1)}, u32[]{:S(2)}, u32[]{:S(2)}) %collective-permute-start.1) | collective-permute-done | bytes 122912 | tf_op jit(solution)/shard_map/ppermute | solution.py:283
  95.6 0.8 collective-permute-done.2.refs_1_
  96.4 0.3 combine_last.1
  96.7 9.8 %all-gather = f32[4,1,128]{2,1,0:T(1,128)S(1)} all-gather(f32[1,1,128]{2,1,0:T(1,128)S(1)} %bitcast.29), channel_id=1, replica_groups=mesh['dp'=32,'chip'=4,'core'=2,'tensor'=4] {'tensor'}, dimensions={0}, use_global_device_ids=true | all-gather | bytes 2560 | tf_op jit(solution)/shard_map/all_gather | solution.py:317
  106.6 0.8 norm.1
  (2 shorter events, 0.0 us)
Async XLA Ops:
  0.0 54.3 %copy-start = (bf16[1,8,40,1408]{3,2,1,0:T(8,128)(2,1)S(1)}, bf16[1,8,40,1408]{3,2,1,0:T(8,128)(2,1)}, u32[]{:S(2)}) copy-start(bf16[1,8,40,1408]{3,2,1,0:T(8,128)(2,1)} %param.9) | copy-start | bytes 2703364
  0.0 53.3 %copy-start.3 = (s32[128,4]{0,1:T(4,128)S(1)}, s32[128,4]{0,1:T(4,128)}, u32[]{:S(2)}) copy-start(s32[128,4]{0,1:T(4,128)} %param.7) | copy-start | bytes 6148
  0.0 53.4 %copy-start.4 = (f32[128,4]{0,1:T(4,128)S(1)}, f32[128,4]{0,1:T(4,128)}, u32[]{:S(2)}) copy-start(f32[128,4]{0,1:T(4,128)} %param.8) | copy-start | bytes 6148
  0.0 53.7 %copy-start.2 = (f32[768]{0:T(1024)S(1)}, f32[768]{0:T(1024)}, u32[]{:S(2)}) copy-start(f32[768]{0:T(1024)} %param.11) | copy-start | bytes 9220
  6.3 67.3 %copy-start.1 = (bf16[128,768]{1,0:T(8,128)(2,1)S(1)}, bf16[128,768]{1,0:T(8,128)(2,1)}, u32[]{:S(2)}) copy-start(bf16[128,768]{1,0:T(8,128)(2,1)} %residual_ref.1) | copy-start | bytes 589828
  20.4 39.2 %all-to-all-start.1 = ((bf16[8,2,40,768]{3,2,1,0:T(8,128)(2,1)}), bf16[8,2,40,768]{3,2,1,0:T(8,128)(2,1)S(1)}, u32[]{:S(2)}, u32[]{:S(2)}) async-start(bf16[8,2,40,768]{3,2,1,0:T(8,128)(2,1)} %bitcast.32), calls=%async_computation.1 | async-start | bytes 1966080 | tf_op jit(solution)/shard_map/all_to_all | solution.py:304
  24.2 49.3 %collective-permute-start = (bf16[2,40,768]{2,1,0:T(8,128)(2,1)S(1)}, bf16[2,40,768]{2,1,0:T(8,128)(2,1)S(1)}, u32[]{:S(2)}, u32[]{:S(2)}) collective-permute-start(bf16[2,40,768]{2,1,0:T(8,128)(2,1)S(1)} %add_groups.3.refs_0_), channel_id=1, source_target_pairs={{0,16},{8,24},{16,0},{24,8},{1,17},{9,25},{17,1},{25,9},{2,18},{10... | collective-permute-start | bytes 368648 | tf_op jit(solution)/shard_map/ppermute | solution.py:283
  59.7 35.9 %collective-permute-start.1 = (bf16[2,40,768]{2,1,0:T(8,128)(2,1)S(1)}, bf16[2,40,768]{2,1,0:T(8,128)(2,1)S(1)}, u32[]{:S(2)}, u32[]{:S(2)}) collective-permute-start(bf16[2,40,768]{2,1,0:T(8,128)(2,1)S(1)} %get-tuple-element.22), channel_id=1, source_target_pairs={{0,24},{8,16},{16,8},{24,0},{1,25},{9,17},{17,9},{25,1},{2,26},{10... | collective-permute-start | bytes 368648 | tf_op jit(solution)/shard_map/ppermute | solution.py:283
  61.6 34.8 %collective-permute-start.2 = (bf16[2,40,768]{2,1,0:T(8,128)(2,1)S(1)}, bf16[2,40,768]{2,1,0:T(8,128)(2,1)S(1)}, u32[]{:S(2)}, u32[]{:S(2)}) collective-permute-start(bf16[2,40,768]{2,1,0:T(8,128)(2,1)S(1)} %get-tuple-element.23), channel_id=1, source_target_pairs={{0,8},{8,0},{16,24},{24,16},{1,9},{9,1},{17,25},{25,17},{2,10},{10... | collective-permute-start | bytes 368648 | tf_op jit(solution)/shard_map/ppermute | solution.py:283
  70.1 12.8 %all-to-all-start.2 = ((bf16[8,1,40,768]{3,2,1,0:T(8,128)(2,1)}), bf16[8,1,40,768]{3,2,1,0:T(8,128)(2,1)S(1)}, u32[]{:S(2)}, u32[]{:S(2)}) async-start(bf16[8,1,40,768]{3,2,1,0:T(8,128)(2,1)} %bitcast.17), calls=%async_computation.2 | async-start | bytes 983040 | tf_op jit(solution)/shard_map/all_to_all | solution.py:304

commit v3 on v2

--- a/solution.py
+++ b/solution.py
@@ -297,7 +297,8 @@
     hidden = expert_hidden.reshape(chips, CORES * capacity, depth)
     weights = w_down[0]
     far, near, here = PARTS
-    far_value, near_value = down(place, hidden, weights, (far, near), groups, DOWN_VMEM_LIMIT)
+    (far_value,) = down(place, hidden, weights, (far,), groups, DOWN_VMEM_LIMIT)
+    (near_value,) = down(place, hidden, weights, (near,), groups, DOWN_VMEM_LIMIT)
 
     def to_tokens(value, part, later=()):
         shape = value.shape

time: 108 us -> 107 us (level)
  blocking collectives: 23.8 us -> 9.87 us
  Pallas kernels: 13.8 us -> 18.7 us
  starting transfers between devices: 46.4 us -> 51 us
  waiting for transfers between devices: 22.5 us -> 26.1 us
    all_to_all x1 -> x0, blocking collectives: 14 us -> none  [to_tokens(): lax.all_to_all(value.reshape(CORES * groups, *shape[2:]), ('core', 'tenso...]
    pallas_call x2 -> x3, Pallas kernels: 11.6 us -> 16.5 us  [down(): pl.pallas_call(functools.partial(down_kernel, parts), in_specs=[pl.BlockS...]
    all_to_all x2 -> x3, starting transfers between devices: 7.05 us -> 11.7 us  [to_tokens(): lax.all_to_all(value.reshape(CORES * groups, *shape[2:]), ('core', 'tenso...]
    all_to_all x2 -> x3, waiting for transfers between devices: 9.04 us -> 12.7 us  [to_tokens(): lax.all_to_all(value.reshape(CORES * groups, *shape[2:]), ('core', 'tenso...]
  transfers between devices with their start and end apart: 5 -> 6, of which waited for: 3 -> 4; matrix products, arithmetic and copies ran while one was open for 1% -> 1% of each run, Pallas kernels for 6% -> 11%
where the time goes in v3:
time: 107 us
  starting transfers between devices  51 us (48%)
  waiting for transfers between devices  26.1 us (24%)
  Pallas kernels  18.7 us (17%)
  blocking collectives  9.87 us (9%)
    ppermute x3, starting transfers between devices, to_chip(): return lax.ppermute(value, 'chip', [(i, i ^ shift) for i in range(chips)])  39.3 us
    pallas_call x3, Pallas kernels, down(): pl.pallas_call(functools.partial(down_kernel, parts), in_specs=[pl.BlockS...  16.5 us
    ppermute x3, waiting for transfers between devices, to_chip(): return lax.ppermute(value, 'chip', [(i, i ^ shift) for i in range(chips)])  13.4 us
    all_to_all x3, waiting for transfers between devices, to_tokens(): lax.all_to_all(value.reshape(CORES * groups, *shape[2:]), ('core', 'tenso...  12.7 us
    all_to_all x3, starting transfers between devices, to_tokens(): lax.all_to_all(value.reshape(CORES * groups, *shape[2:]), ('core', 'tenso...  11.7 us
    all_gather x1, blocking collectives, body(): square_parts = lax.all_gather(squares, 'tensor', axis=0, tiled=True)  9.87 us
  transfers between devices with their start and end apart: 6, of which 4 were waited for; matrix products, arithmetic and copies ran while one was open for 1% of the time, Pallas kernels for 11%

profile of v3, /device:TPU:6, one launch (start us, length us, event | category | flops | bytes accessed | tf_op | source)
XLA Modules:
  0.0 106.5 jit_solution(4179489608645620068)
XLA Ops:
  0.0 5.4 %down_rows.3 = bf16[2,4,1,40,768]{4,3,2,1,0:T(8,128)(2,1)} custom-call(s32[1]{0:T(128)} %bitcast.8.place_ref, bf16[4,80,1408]{2,1,0:T(8,128)(2,1)} %bitcast.23, bf16[1408,3072]{1,0:T(8,128)(2,1)} %bitcast.31), custom_call_target="tpu_custom_call" | custom-call | flops 692060160 | bytes 9367552 | tf_op jit(solution)/shard_map/down_rows/pallas_call | solution.py:149
  5.5 0.0 copy-start.3
  5.5 0.0 copy-start.4
  5.5 0.0 copy-start.2
  5.5 0.0 copy-start
  5.5 4.6 %all-to-all-start = ((bf16[8,1,40,768]{3,2,1,0:T(8,128)(2,1)}), bf16[8,1,40,768]{3,2,1,0:T(8,128)(2,1)S(1)}, u32[]{:S(2)}, u32[]{:S(2)}) async-start(bf16[8,1,40,768]{3,2,1,0:T(8,128)(2,1)} %bitcast.35), calls=%async_computation | async-start | bytes 983040 | tf_op jit(solution)/shard_map/all_to_all | solution.py:305
  10.1 5.7 %down_rows.4 = bf16[2,4,2,40,768]{4,3,2,1,0:T(8,128)(2,1)} custom-call(s32[1]{0:T(128)} %bitcast.8.place_ref, bf16[4,80,1408]{2,1,0:T(8,128)(2,1)} %bitcast.24, bf16[1408,3072]{1,0:T(8,128)(2,1)} %bitcast.32), custom_call_target="tpu_custom_call" | custom-call | flops 1384120320 | bytes 10084352 | tf_op jit(solution)/shard_map/down_rows/pallas_call | solution.py:149
  15.9 0.0 copy-start.1
  15.9 3.6 %all-to-all-done = bf16[8,1,40,768]{3,2,1,0:T(8,128)(2,1)S(1)} async-done(((bf16[8,1,40,768]{3,2,1,0:T(8,128)(2,1)}), bf16[8,1,40,768]{3,2,1,0:T(8,128)(2,1)S(1)}, u32[]{:S(2)}, u32[]{:S(2)}) %all-to-all-start) | async-done | bytes 491552 | tf_op jit(solution)/shard_map/all_to_all | solution.py:305
  19.5 3.6 %all-to-all-start.1 = ((bf16[8,2,40,768]{3,2,1,0:T(8,128)(2,1)}), bf16[8,2,40,768]{3,2,1,0:T(8,128)(2,1)S(1)}, u32[]{:S(2)}, u32[]{:S(2)}) async-start(bf16[8,2,40,768]{3,2,1,0:T(8,128)(2,1)} %bitcast.34), calls=%async_computation.1 | async-start | bytes 1966080 | tf_op jit(solution)/shard_map/all_to_all | solution.py:305
  23.1 0.1 stack.42
  23.2 0.1 add_multiply_fusion
  23.2 0.1 iota_add_fusion
  23.3 0.1 add_groups.3.refs_0_
  23.4 29.0 %collective-permute-start = (bf16[2,40,768]{2,1,0:T(8,128)(2,1)S(1)}, bf16[2,40,768]{2,1,0:T(8,128)(2,1)S(1)}, u32[]{:S(2)}, u32[]{:S(2)}) collective-permute-start(bf16[2,40,768]{2,1,0:T(8,128)(2,1)S(1)} %add_groups.3.refs_0_), channel_id=1, source_target_pairs={{0,16},{8,24},{16,0},{24,8},{1,17},{9,25},{17,1},{25,9},{2,18},{10... | collective-permute-start | bytes 368648 | tf_op jit(solution)/shard_map/ppermute | solution.py:283
  52.4 0.1 iota_add_fusion.1
  52.4 0.0 copy-done.3
  52.4 0.1 copy.11.ids_ref
  52.5 0.0 copy-done.4
  52.5 0.1 copy.12.gate_ref
  52.7 0.1 add.62.refs_0_
  52.7 0.1 add.69.refs_1_
  52.8 0.0 copy-done.2
  52.8 0.6 routing_tables.1
  53.4 0.0 copy-done
  53.4 5.3 %down_rows.5.refs_0_ = bf16[2,4,1,40,768]{4,3,2,1,0:T(8,128)(2,1)} custom-call(s32[1]{0:T(128)} %bitcast.8.place_ref, bf16[4,80,1408]{2,1,0:T(8,128)(2,1)S(1)} %bitcast.25, bf16[1408,3072]{1,0:T(8,128)(2,1)} %bitcast.33, bf16[2,40,768]{2,1,0:T(8,128)(2,1)S(1)} %add_groups.3.refs_0_), custom_call_target="tpu_custom_call" | custom-call | flops 692060160 | bytes 9367552 | tf_op jit(solution)/shard_map/down_rows/pallas_call | solution.py:149
  58.7 0.0 all-to-all-done.1
  58.7 0.1 add_groups.4
  58.9 1.9 %collective-permute-start.1 = (bf16[2,40,768]{2,1,0:T(8,128)(2,1)S(1)}, bf16[2,40,768]{2,1,0:T(8,128)(2,1)S(1)}, u32[]{:S(2)}, u32[]{:S(2)}) collective-permute-start(bf16[2,40,768]{2,1,0:T(8,128)(2,1)S(1)} %get-tuple-element.18), channel_id=1, source_target_pairs={{0,24},{8,16},{16,8},{24,0},{1,25},{9,17},{17,9},{25,1},{2,26},{10... | collective-permute-start | bytes 368648 | tf_op jit(solution)/shard_map/ppermute | solution.py:283
  60.8 8.4 %collective-permute-start.2 = (bf16[2,40,768]{2,1,0:T(8,128)(2,1)S(1)}, bf16[2,40,768]{2,1,0:T(8,128)(2,1)S(1)}, u32[]{:S(2)}, u32[]{:S(2)}) collective-permute-start(bf16[2,40,768]{2,1,0:T(8,128)(2,1)S(1)} %get-tuple-element.19), channel_id=1, source_target_pairs={{0,8},{8,0},{16,24},{24,16},{1,9},{9,1},{17,25},{25,17},{2,10},{10... | collective-permute-start | bytes 368648 | tf_op jit(solution)/shard_map/ppermute | solution.py:283
  69.2 3.5 %all-to-all-start.2 = ((bf16[8,1,40,768]{3,2,1,0:T(8,128)(2,1)}), bf16[8,1,40,768]{3,2,1,0:T(8,128)(2,1)S(1)}, u32[]{:S(2)}, u32[]{:S(2)}) async-start(bf16[8,1,40,768]{3,2,1,0:T(8,128)(2,1)} %bitcast.17), calls=%async_computation.2 | async-start | bytes 983040 | tf_op jit(solution)/shard_map/all_to_all | solution.py:305
  72.7 0.0 collective-permute-done.refs_0_
  72.7 0.0 copy-done.1
  72.7 0.2 combine_first.1.begun_ref
  73.0 9.0 %all-to-all-done.2 = bf16[8,1,40,768]{3,2,1,0:T(8,128)(2,1)S(1)} async-done(((bf16[8,1,40,768]{3,2,1,0:T(8,128)(2,1)}), bf16[8,1,40,768]{3,2,1,0:T(8,128)(2,1)S(1)}, u32[]{:S(2)}, u32[]{:S(2)}) %all-to-all-start.2) | async-done | bytes 491552 | tf_op jit(solution)/shard_map/all_to_all | solution.py:305
  82.0 0.1 add_groups.5.refs_2_
  82.1 12.4 %collective-permute-done.1.refs_0_ = bf16[2,40,768]{2,1,0:T(8,128)(2,1)S(1)} collective-permute-done((bf16[2,40,768]{2,1,0:T(8,128)(2,1)S(1)}, bf16[2,40,768]{2,1,0:T(8,128)(2,1)S(1)}, u32[]{:S(2)}, u32[]{:S(2)}) %collective-permute-start.1) | collective-permute-done | bytes 122912 | tf_op jit(solution)/shard_map/ppermute | solution.py:283
  94.5 1.0 collective-permute-done.2.refs_1_
  95.5 0.3 combine_last.1
  95.9 9.9 %all-gather = f32[4,1,128]{2,1,0:T(1,128)S(1)} all-gather(f32[1,1,128]{2,1,0:T(1,128)S(1)} %bitcast.30), channel_id=1, replica_groups=mesh['dp'=32,'chip'=4,'core'=2,'tensor'=4] {'tensor'}, dimensions={0}, use_global_device_ids=true | all-gather | bytes 2560 | tf_op jit(solution)/shard_map/all_gather | solution.py:318
  105.7 0.8 norm.1
  (2 shorter events, 0.0 us)
Async XLA Ops:
  5.5 47.0 %copy-start.3 = (s32[128,4]{0,1:T(4,128)S(1)}, s32[128,4]{0,1:T(4,128)}, u32[]{:S(2)}) copy-start(s32[128,4]{0,1:T(4,128)} %param.7) | copy-start | bytes 6148
  5.5 47.1 %copy-start.4 = (f32[128,4]{0,1:T(4,128)S(1)}, f32[128,4]{0,1:T(4,128)}, u32[]{:S(2)}) copy-start(f32[128,4]{0,1:T(4,128)} %param.8) | copy-start | bytes 6148
  5.5 47.3 %copy-start.2 = (f32[768]{0:T(1024)S(1)}, f32[768]{0:T(1024)}, u32[]{:S(2)}) copy-start(f32[768]{0:T(1024)} %param.11) | copy-start | bytes 9220
  5.5 47.9 %copy-start = (bf16[1,8,40,1408]{3,2,1,0:T(8,128)(2,1)S(1)}, bf16[1,8,40,1408]{3,2,1,0:T(8,128)(2,1)}, u32[]{:S(2)}) copy-start(bf16[1,8,40,1408]{3,2,1,0:T(8,128)(2,1)} %param.9) | copy-start | bytes 2703364
  5.5 14.0 %all-to-all-start = ((bf16[8,1,40,768]{3,2,1,0:T(8,128)(2,1)}), bf16[8,1,40,768]{3,2,1,0:T(8,128)(2,1)S(1)}, u32[]{:S(2)}, u32[]{:S(2)}) async-start(bf16[8,1,40,768]{3,2,1,0:T(8,128)(2,1)} %bitcast.35), calls=%async_computation | async-start | bytes 983040 | tf_op jit(solution)/shard_map/all_to_all | solution.py:305
  15.9 56.9 %copy-start.1 = (bf16[128,768]{1,0:T(8,128)(2,1)S(1)}, bf16[128,768]{1,0:T(8,128)(2,1)}, u32[]{:S(2)}) copy-start(bf16[128,768]{1,0:T(8,128)(2,1)} %residual_ref.1) | copy-start | bytes 589828
  19.5 39.2 %all-to-all-start.1 = ((bf16[8,2,40,768]{3,2,1,0:T(8,128)(2,1)}), bf16[8,2,40,768]{3,2,1,0:T(8,128)(2,1)S(1)}, u32[]{:S(2)}, u32[]{:S(2)}) async-start(bf16[8,2,40,768]{3,2,1,0:T(8,128)(2,1)} %bitcast.34), calls=%async_computation.1 | async-start | bytes 1966080 | tf_op jit(solution)/shard_map/all_to_all | solution.py:305
  23.4 49.3 %collective-permute-start = (bf16[2,40,768]{2,1,0:T(8,128)(2,1)S(1)}, bf16[2,40,768]{2,1,0:T(8,128)(2,1)S(1)}, u32[]{:S(2)}, u32[]{:S(2)}) collective-permute-start(bf16[2,40,768]{2,1,0:T(8,128)(2,1)S(1)} %add_groups.3.refs_0_), channel_id=1, source_target_pairs={{0,16},{8,24},{16,0},{24,8},{1,17},{9,25},{17,1},{25,9},{2,18},{10... | collective-permute-start | bytes 368648 | tf_op jit(solution)/shard_map/ppermute | solution.py:283
  58.9 35.6 %collective-permute-start.1 = (bf16[2,40,768]{2,1,0:T(8,128)(2,1)S(1)}, bf16[2,40,768]{2,1,0:T(8,128)(2,1)S(1)}, u32[]{:S(2)}, u32[]{:S(2)}) collective-permute-start(bf16[2,40,768]{2,1,0:T(8,128)(2,1)S(1)} %get-tuple-element.18), channel_id=1, source_target_pairs={{0,24},{8,16},{16,8},{24,0},{1,25},{9,17},{17,9},{25,1},{2,26},{10... | collective-permute-start | bytes 368648 | tf_op jit(solution)/shard_map/ppermute | solution.py:283
  60.8 34.7 %collective-permute-start.2 = (bf16[2,40,768]{2,1,0:T(8,128)(2,1)S(1)}, bf16[2,40,768]{2,1,0:T(8,128)(2,1)S(1)}, u32[]{:S(2)}, u32[]{:S(2)}) collective-permute-start(bf16[2,40,768]{2,1,0:T(8,128)(2,1)S(1)} %get-tuple-element.19), channel_id=1, source_target_pairs={{0,8},{8,0},{16,24},{24,16},{1,9},{9,1},{17,25},{25,17},{2,10},{10... | collective-permute-start | bytes 368648 | tf_op jit(solution)/shard_map/ppermute | solution.py:283
  69.2 12.8 %all-to-all-start.2 = ((bf16[8,1,40,768]{3,2,1,0:T(8,128)(2,1)}), bf16[8,1,40,768]{3,2,1,0:T(8,128)(2,1)S(1)}, u32[]{:S(2)}, u32[]{:S(2)}) async-start(bf16[8,1,40,768]{3,2,1,0:T(8,128)(2,1)} %bitcast.17), calls=%async_computation.2 | async-start | bytes 983040 | tf_op jit(solution)/shard_map/all_to_all | solution.py:305

commit v4 on v3

--- a/solution.py
+++ b/solution.py
@@ -298,7 +298,9 @@
     weights = w_down[0]
     far, near, here = PARTS
     (far_value,) = down(place, hidden, weights, (far,), groups, DOWN_VMEM_LIMIT)
-    (near_value,) = down(place, hidden, weights, (near,), groups, DOWN_VMEM_LIMIT)
+    (near_value,) = down(
+        place, hidden, weights, (near,), groups, DOWN_VMEM_LIMIT, table_first[:1]
+    )
 
     def to_tokens(value, part, later=()):
         shape = value.shape

time: 107 us -> 106 us (level)
  waiting for transfers between devices: 26.1 us -> 23.2 us
  starting transfers between devices: 51 us -> 52.2 us
    all_to_all x3, waiting for transfers between devices: 12.7 us -> 10.7 us  [to_tokens(): lax.all_to_all(value.reshape(CORES * groups, *shape[2:]), ('core', 'tenso...]
    ppermute x3, starting transfers between devices: 39.3 us -> 40.6 us  [to_chip(): return lax.ppermute(value, 'chip', [(i, i ^ shift) for i in range(chips)])]
where the time goes in v4:
time: 106 us; the launch traced here: 105 us
  starting transfers between devices  52.2 us (49%)
  waiting for transfers between devices  23.2 us (22%)
  Pallas kernels  18.7 us (18%)
  blocking collectives  9.8 us (9%)
  local copies, waits for them, and re-layouts  1.12 us (1%)
    ppermute x3, starting transfers between devices, to_chip(): return lax.ppermute(value, 'chip', [(i, i ^ shift) for i in range(chips)])  40.6 us
    pallas_call x3, Pallas kernels, down(): pl.pallas_call(functools.partial(down_kernel, parts), in_specs=[pl.BlockS...  16.5 us
    ppermute x3, waiting for transfers between devices, to_chip(): return lax.ppermute(value, 'chip', [(i, i ^ shift) for i in range(chips)])  12.4 us
    all_to_all x3, starting transfers between devices, to_tokens(): lax.all_to_all(value.reshape(CORES * groups, *shape[2:]), ('core', 'tenso...  11.7 us
    all_to_all x3, waiting for transfers between devices, to_tokens(): lax.all_to_all(value.reshape(CORES * groups, *shape[2:]), ('core', 'tenso...  10.7 us
    all_gather x1, blocking collectives, body(): square_parts = lax.all_gather(squares, 'tensor', axis=0, tiled=True)  9.8 us
  transfers between devices with their start and end apart: 6, of which 4 were waited for; matrix products, arithmetic and copies ran while one was open for 1% of the time, Pallas kernels for 11%

profile of v4, /device:TPU:6, one launch (start us, length us, event | category | flops | bytes accessed | tf_op | source)
XLA Modules:
  0.0 105.5 jit_solution(14468877614953556072)
XLA Ops:
  0.0 0.0 copy-start.5
  0.0 0.0 copy-start.6
  0.0 5.5 %down_rows.3 = bf16[2,4,1,40,768]{4,3,2,1,0:T(8,128)(2,1)} custom-call(s32[1]{0:T(128)} %bitcast.8.place_ref, bf16[4,80,1408]{2,1,0:T(8,128)(2,1)} %bitcast.23, bf16[1408,3072]{1,0:T(8,128)(2,1)} %bitcast.31), custom_call_target="tpu_custom_call" | custom-call | flops 692060160 | bytes 9367552 | tf_op jit(solution)/shard_map/down_rows/pallas_call | solution.py:149
  5.5 0.0 copy-start.4
  5.5 0.0 copy-start
  5.5 4.6 %all-to-all-start = ((bf16[8,1,40,768]{3,2,1,0:T(8,128)(2,1)}), bf16[8,1,40,768]{3,2,1,0:T(8,128)(2,1)S(1)}, u32[]{:S(2)}, u32[]{:S(2)}) async-start(bf16[8,1,40,768]{3,2,1,0:T(8,128)(2,1)} %bitcast.35), calls=%async_computation | async-start | bytes 983040 | tf_op jit(solution)/shard_map/all_to_all | solution.py:307
  10.1 0.1 add_multiply_fusion
  10.2 0.1 iota_add_fusion.1
  10.3 0.1 stack.42
  10.4 0.0 copy-done.5
  10.4 0.1 copy.11.ids_ref
  10.5 0.0 copy-done.6
  10.5 0.1 copy.12.gate_ref
  10.6 0.1 add.62.refs_0_
  10.7 0.1 iota_add_fusion
  10.7 0.1 add.69.refs_1_
  10.8 0.6 routing_tables.1
  11.4 0.0 copy-start.1
  11.4 0.6 copy-done.1
  12.0 5.8 %down_rows.4 = bf16[2,4,2,40,768]{4,3,2,1,0:T(8,128)(2,1)} custom-call(s32[1]{0:T(128)} %bitcast.8.place_ref, bf16[4,80,1408]{2,1,0:T(8,128)(2,1)} %bitcast.24, bf16[1408,3072]{1,0:T(8,128)(2,1)} %bitcast.32, bf16[128,80]{1,0:T(8,128)(2,1)} %copy-done.1), custom_call_target="tpu_custom_call" | custom-call | flops 1384120320 | bytes 10084352 | tf_op jit(solution)/shard_map/down_rows/pallas_call | solution.py:149
  17.8 0.0 copy-start.2
  17.8 0.0 copy-start.3
  17.8 1.7 %all-to-all-done = bf16[8,1,40,768]{3,2,1,0:T(8,128)(2,1)S(1)} async-done(((bf16[8,1,40,768]{3,2,1,0:T(8,128)(2,1)}), bf16[8,1,40,768]{3,2,1,0:T(8,128)(2,1)S(1)}, u32[]{:S(2)}, u32[]{:S(2)}) %all-to-all-start) | async-done | bytes 491552 | tf_op jit(solution)/shard_map/all_to_all | solution.py:307
  19.5 3.6 %all-to-all-start.1 = ((bf16[8,2,40,768]{3,2,1,0:T(8,128)(2,1)}), bf16[8,2,40,768]{3,2,1,0:T(8,128)(2,1)S(1)}, u32[]{:S(2)}, u32[]{:S(2)}) async-start(bf16[8,2,40,768]{3,2,1,0:T(8,128)(2,1)} %bitcast.34), calls=%async_computation.1 | async-start | bytes 1966080 | tf_op jit(solution)/shard_map/all_to_all | solution.py:307
  23.1 0.1 add_groups.3.refs_0_
  23.1 29.0 %collective-permute-start = (bf16[2,40,768]{2,1,0:T(8,128)(2,1)S(1)}, bf16[2,40,768]{2,1,0:T(8,128)(2,1)S(1)}, u32[]{:S(2)}, u32[]{:S(2)}) collective-permute-start(bf16[2,40,768]{2,1,0:T(8,128)(2,1)S(1)} %add_groups.3.refs_0_), channel_id=1, source_target_pairs={{0,16},{8,24},{16,0},{24,8},{1,17},{9,25},{17,1},{25,9},{2,18},{10... | collective-permute-start | bytes 368648 | tf_op jit(solution)/shard_map/ppermute | solution.py:283
  52.1 0.0 copy-done.4
  52.1 0.0 copy-done
  52.1 5.3 %down_rows.5.refs_0_ = bf16[2,4,1,40,768]{4,3,2,1,0:T(8,128)(2,1)} custom-call(s32[1]{0:T(128)} %bitcast.8.place_ref, bf16[4,80,1408]{2,1,0:T(8,128)(2,1)S(1)} %bitcast.25, bf16[1408,3072]{1,0:T(8,128)(2,1)} %bitcast.33, bf16[2,40,768]{2,1,0:T(8,128)(2,1)S(1)} %add_groups.3.refs_0_), custom_call_target="tpu_custom_call" | custom-call | flops 692060160 | bytes 9367552 | tf_op jit(solution)/shard_map/down_rows/pallas_call | solution.py:149
  57.4 0.0 all-to-all-done.1
  57.5 0.1 add_groups.4
  57.6 3.2 %collective-permute-start.1 = (bf16[2,40,768]{2,1,0:T(8,128)(2,1)S(1)}, bf16[2,40,768]{2,1,0:T(8,128)(2,1)S(1)}, u32[]{:S(2)}, u32[]{:S(2)}) collective-permute-start(bf16[2,40,768]{2,1,0:T(8,128)(2,1)S(1)} %get-tuple-element.18), channel_id=1, source_target_pairs={{0,24},{8,16},{16,8},{24,0},{1,25},{9,17},{17,9},{25,1},{2,26},{10... | collective-permute-start | bytes 368648 | tf_op jit(solution)/shard_map/ppermute | solution.py:283
  60.8 8.4 %collective-permute-start.2 = (bf16[2,40,768]{2,1,0:T(8,128)(2,1)S(1)}, bf16[2,40,768]{2,1,0:T(8,128)(2,1)S(1)}, u32[]{:S(2)}, u32[]{:S(2)}) collective-permute-start(bf16[2,40,768]{2,1,0:T(8,128)(2,1)S(1)} %get-tuple-element.19), channel_id=1, source_target_pairs={{0,8},{8,0},{16,24},{24,16},{1,9},{9,1},{17,25},{25,17},{2,10},{10... | collective-permute-start | bytes 368648 | tf_op jit(solution)/shard_map/ppermute | solution.py:283
  69.2 3.5 %all-to-all-start.2 = ((bf16[8,1,40,768]{3,2,1,0:T(8,128)(2,1)}), bf16[8,1,40,768]{3,2,1,0:T(8,128)(2,1)S(1)}, u32[]{:S(2)}, u32[]{:S(2)}) async-start(bf16[8,1,40,768]{3,2,1,0:T(8,128)(2,1)} %bitcast.17), calls=%async_computation.2 | async-start | bytes 983040 | tf_op jit(solution)/shard_map/all_to_all | solution.py:307
  72.7 0.0 collective-permute-done.refs_0_
  72.7 0.0 copy-done.2
  72.7 0.0 copy-done.3
  72.7 0.2 combine_first.1.begun_ref
  73.0 9.0 %all-to-all-done.2 = bf16[8,1,40,768]{3,2,1,0:T(8,128)(2,1)S(1)} async-done(((bf16[8,1,40,768]{3,2,1,0:T(8,128)(2,1)}), bf16[8,1,40,768]{3,2,1,0:T(8,128)(2,1)S(1)}, u32[]{:S(2)}, u32[]{:S(2)}) %all-to-all-start.2) | async-done | bytes 491552 | tf_op jit(solution)/shard_map/all_to_all | solution.py:307
  82.0 0.1 add_groups.5.refs_2_
  82.1 11.4 %collective-permute-done.1.refs_0_ = bf16[2,40,768]{2,1,0:T(8,128)(2,1)S(1)} collective-permute-done((bf16[2,40,768]{2,1,0:T(8,128)(2,1)S(1)}, bf16[2,40,768]{2,1,0:T(8,128)(2,1)S(1)}, u32[]{:S(2)}, u32[]{:S(2)}) %collective-permute-start.1) | collective-permute-done | bytes 122912 | tf_op jit(solution)/shard_map/ppermute | solution.py:283
  93.5 1.0 collective-permute-done.2.refs_1_
  94.5 0.3 combine_last.1
  94.9 9.8 %all-gather = f32[4,1,128]{2,1,0:T(1,128)S(1)} all-gather(f32[1,1,128]{2,1,0:T(1,128)S(1)} %bitcast.30), channel_id=1, replica_groups=mesh['dp'=32,'chip'=4,'core'=2,'tensor'=4] {'tensor'}, dimensions={0}, use_global_device_ids=true | all-gather | bytes 2560 | tf_op jit(solution)/shard_map/all_gather | solution.py:320
  104.7 0.8 norm.1
  (2 shorter events, 0.0 us)
Async XLA Ops:
  0.0 10.4 %copy-start.5 = (s32[128,4]{0,1:T(4,128)S(1)}, s32[128,4]{0,1:T(4,128)}, u32[]{:S(2)}) copy-start(s32[128,4]{0,1:T(4,128)} %param.7) | copy-start | bytes 6148
  0.0 10.5 %copy-start.6 = (f32[128,4]{0,1:T(4,128)S(1)}, f32[128,4]{0,1:T(4,128)}, u32[]{:S(2)}) copy-start(f32[128,4]{0,1:T(4,128)} %param.8) | copy-start | bytes 6148
  5.5 46.6 %copy-start.4 = (f32[768]{0:T(1024)S(1)}, f32[768]{0:T(1024)}, u32[]{:S(2)}) copy-start(f32[768]{0:T(1024)} %param.11) | copy-start | bytes 9220
  5.5 46.6 %copy-start = (bf16[1,8,40,1408]{3,2,1,0:T(8,128)(2,1)S(1)}, bf16[1,8,40,1408]{3,2,1,0:T(8,128)(2,1)}, u32[]{:S(2)}) copy-start(bf16[1,8,40,1408]{3,2,1,0:T(8,128)(2,1)} %param.9) | copy-start | bytes 2703364
  5.5 14.0 %all-to-all-start = ((bf16[8,1,40,768]{3,2,1,0:T(8,128)(2,1)}), bf16[8,1,40,768]{3,2,1,0:T(8,128)(2,1)S(1)}, u32[]{:S(2)}, u32[]{:S(2)}) async-start(bf16[8,1,40,768]{3,2,1,0:T(8,128)(2,1)} %bitcast.35), calls=%async_computation | async-start | bytes 983040 | tf_op jit(solution)/shard_map/all_to_all | solution.py:307
  11.4 0.6 copy-start.1
  17.8 54.9 %copy-start.2 = (bf16[128,80]{1,0:T(8,128)(2,1)S(1)}, bf16[128,80]{1,0:T(8,128)(2,1)}, u32[]{:S(2)}) copy-start(bf16[128,80]{1,0:T(8,128)(2,1)} %copy-done.1) | copy-start | bytes 61444
  17.8 54.9 %copy-start.3 = (bf16[128,768]{1,0:T(8,128)(2,1)S(1)}, bf16[128,768]{1,0:T(8,128)(2,1)}, u32[]{:S(2)}) copy-start(bf16[128,768]{1,0:T(8,128)(2,1)} %residual_ref.1) | copy-start | bytes 589828
  19.5 38.0 %all-to-all-start.1 = ((bf16[8,2,40,768]{3,2,1,0:T(8,128)(2,1)}), bf16[8,2,40,768]{3,2,1,0:T(8,128)(2,1)S(1)}, u32[]{:S(2)}, u32[]{:S(2)}) async-start(bf16[8,2,40,768]{3,2,1,0:T(8,128)(2,1)} %bitcast.34), calls=%async_computation.1 | async-start | bytes 1966080 | tf_op jit(solution)/shard_map/all_to_all | solution.py:307
  23.1 49.6 %collective-permute-start = (bf16[2,40,768]{2,1,0:T(8,128)(2,1)S(1)}, bf16[2,40,768]{2,1,0:T(8,128)(2,1)S(1)}, u32[]{:S(2)}, u32[]{:S(2)}) collective-permute-start(bf16[2,40,768]{2,1,0:T(8,128)(2,1)S(1)} %add_groups.3.refs_0_), channel_id=1, source_target_pairs={{0,16},{8,24},{16,0},{24,8},{1,17},{9,25},{17,1},{25,9},{2,18},{10... | collective-permute-start | bytes 368648 | tf_op jit(solution)/shard_map/ppermute | solution.py:283
  57.6 35.9 %collective-permute-start.1 = (bf16[2,40,768]{2,1,0:T(8,128)(2,1)S(1)}, bf16[2,40,768]{2,1,0:T(8,128)(2,1)S(1)}, u32[]{:S(2)}, u32[]{:S(2)}) collective-permute-start(bf16[2,40,768]{2,1,0:T(8,128)(2,1)S(1)} %get-tuple-element.18), channel_id=1, source_target_pairs={{0,24},{8,16},{16,8},{24,0},{1,25},{9,17},{17,9},{25,1},{2,26},{10... | collective-permute-start | bytes 368648 | tf_op jit(solution)/shard_map/ppermute | solution.py:283
  60.8 33.8 %collective-permute-start.2 = (bf16[2,40,768]{2,1,0:T(8,128)(2,1)S(1)}, bf16[2,40,768]{2,1,0:T(8,128)(2,1)S(1)}, u32[]{:S(2)}, u32[]{:S(2)}) collective-permute-start(bf16[2,40,768]{2,1,0:T(8,128)(2,1)S(1)} %get-tuple-element.19), channel_id=1, source_target_pairs={{0,8},{8,0},{16,24},{24,16},{1,9},{9,1},{17,25},{25,17},{2,10},{10... | collective-permute-start | bytes 368648 | tf_op jit(solution)/shard_map/ppermute | solution.py:283
  69.2 12.8 %all-to-all-start.2 = ((bf16[8,1,40,768]{3,2,1,0:T(8,128)(2,1)}), bf16[8,1,40,768]{3,2,1,0:T(8,128)(2,1)S(1)}, u32[]{:S(2)}, u32[]{:S(2)}) async-start(bf16[8,1,40,768]{3,2,1,0:T(8,128)(2,1)} %bitcast.17), calls=%async_computation.2 | async-start | bytes 983040 | tf_op jit(solution)/shard_map/all_to_all | solution.py:307
